TPU v7x, 32 devices: a whole 2x2x4 slice. The times are simulated.
32 devices in a mesh: prompt: 2 (over x), feat: 16 (over z, y, core).
Axes of the slice: x: 2, y: 2, z: 4, core: 2. Of those that a mesh axis runs over, the one named last changes fastest.
Arguments:
- decoder: bfloat16 [4096, 5376], P('feat'), may hold values from -0.078125 to 0.078125
- encoder: bfloat16 [12288, 5376], P(('feat', 'prompt')), may hold values from -6 to 6
- row_ids: int32 [2, 256], P('prompt', 'feat'), may hold values from 0 to 255
- counts: int32 [2, 16], P('prompt'), may hold values from 1 to 16, 153 in all within a row
- activity: float32 [2, 256], P('prompt'), may hold values from 0.25 to 4
Outputs:
- edges: bfloat16 [2, 256, 12288], P('prompt', None, 'feat')
Inputs may be any that keep to these rules, and one draw needn't show every extreme that they name: counts of one prompt sum to 153; some owner of each prompt holds exactly 16.
All inputs are finite; a program needn't handle non-finite values.
Results may differ from a plain program's by a relative error of at most 0.001.
Values may be sent and summed in bfloat16 or wider, within the bound.
A program may use at most 64 MiB of HBM per device.

v0:
```python
import jax
import jax.numpy as jnp
from jax import lax
from jax.sharding import PartitionSpec as P


def per_device(decoder, encoder, row_ids, counts, activity):
    slot_count = row_ids.shape[1]
    owner_index = lax.axis_index("feat")
    picked_rows = jnp.take(decoder, row_ids[0], axis=0)
    live_count = lax.dynamic_index_in_dim(counts[0], owner_index, 0, keepdims=False)
    live_slots = jnp.arange(slot_count, dtype=jnp.int32) < live_count
    source_rows = jnp.where(live_slots[:, None], picked_rows, jnp.zeros((), picked_rows.dtype))
    weights = activity[0]
    whole_rows = lax.all_gather(source_rows, "feat", axis=0, tiled=True)
    products = lax.dot_general(
        whole_rows,
        lax.all_gather(encoder, "prompt", axis=0, tiled=True),
        (((1,), (1,)), ((), ())),
        preferred_element_type=jnp.float32,
    )
    edges = (weights[:, None] * products).astype(jnp.bfloat16)
    return edges[None]


def solution(mesh):
    in_specs = (
        P("feat", None),
        P(("feat", "prompt"), None),
        P("prompt", "feat"),
        P("prompt", None),
        P("prompt", None),
    )
    out_specs = P("prompt", None, "feat")
    return jax.shard_map(
        per_device, mesh=mesh, in_specs=in_specs, out_specs=out_specs, check_vma=False
    )
```

profile of v0, /device:TPU:0, one launch (start us, length us, event | category | flops | bytes accessed | tf_op | source)
XLA Modules:
  0.0 174.7 jit_solution(10127806332455465472)
XLA Ops:
  6.5 0.0 copy-start
  6.5 0.0 all-gather.3.cloned.1.call-start
  6.5 0.8 fusion.2
  7.3 1.3 constant_dynamic-slice_fusion
  8.6 1.3 compare_and_fusion
  9.9 0.0 copy-done
  9.9 0.0 copy-start.1
  10.0 0.7 gather_fusion
  10.6 0.8 select_select_fusion
  11.4 0.0 all-gather.3.cloned.1.call-update
  11.4 0.0 all-gather.5.cloned.1.call-start
  11.4 0.7 all-gather.5.cloned.1.call-update
  12.2 45.8 %all-gather.3.cloned.1.call-done = bf16[256,5376]{1,0:T(8,128)(2,1)} async-done(((bf16[16,5376]{1,0:T(8,128)(2,1)}), bf16[256,5376]{1,0:T(8,128)(2,1)}) %all-gather.3.cloned.1.call-update) | async-done | bytes 2752528 | tf_op jit(solution)/shard_map/all_gather | solution.py:15
  58.0 102.6 %all-gather.5.cloned.1.call-done = bf16[768,5376]{1,0:T(8,128)(2,1)} async-done(((bf16[384,5376]{1,0:T(8,128)(2,1)}), bf16[768,5376]{1,0:T(8,128)(2,1)}) %all-gather.5.cloned.1.call-update) | async-done | bytes 8257552 | tf_op jit(solution)/shard_map/all_gather | solution.py:18
  160.6 0.0 copy-done.1
  160.6 7.3 %fusion.1 = bf16[1,256,768]{2,1,0:T(8,128)(2,1)} fusion(bf16[256,5376]{1,0:T(8,128)(2,1)} %all-gather.3.cloned.1.call-done, bf16[768,5376]{1,0:T(8,128)(2,1)} %all-gather.5.cloned.1.call-done, f32[256]{0:T(256)S(1)} %bitcast.12), kind=kOutput, calls=%fused_computation.3 | convolution fusion | flops 2114322432 | bytes 11404288 | tf_op jit(solution)/shard_map/dot_general | solution.py:16
  (1 shorter events, 0.0 us)
Async XLA Ops:
  6.5 3.4 %copy-start = (bf16[256,5376]{1,0:T(8,128)(2,1)S(1)}, bf16[256,5376]{1,0:T(8,128)(2,1)}, u32[]{:S(2)}) copy-start(bf16[256,5376]{1,0:T(8,128)(2,1)} %param.5) | copy-start | bytes 8257540
  6.5 51.4 %all-gather.3.cloned.1.call-start = ((), (), s32[]{:S(2)}) async-start(), calls=%async_computation | async-start | bytes 2924544 | tf_op jit(solution)/shard_map/all_gather | solution.py:15
  9.9 150.7 %copy-start.1 = (f32[1,256]{1,0:T(1,128)S(1)}, f32[1,256]{1,0:T(1,128)}, u32[]{:S(2)}) copy-start(f32[1,256]{1,0:T(1,128)} %param.9) | copy-start | bytes 3076
  11.4 149.2 %all-gather.5.cloned.1.call-start = ((), (), s32[]{:S(2)}) async-start(), calls=%async_computation.1 | async-start | bytes 12386304 | tf_op jit(solution)/shard_map/all_gather | solution.py:18
Sparse Core Ops, SparseCore 0:
  11.5 46.4 all-gather.2
  59.5 101.0 all-gather.4
where the time goes:
time: 175 us
  waiting for transfers between devices  149 us (85%)
  between operations  13.4 us (8%)
  matrix products  7.26 us (4%)
  other arithmetic  2.88 us (2%)
  local copies, waits for them, and re-layouts  1.93 us (1%)
    all_gather x1, waiting for transfers between devices, per_device(): lax.all_gather(encoder, 'prompt', axis=0, tiled=True)  103 us
    all_gather x1, waiting for transfers between devices, per_device(): whole_rows = lax.all_gather(source_rows, 'feat', axis=0, tiled=True)  45.8 us
    dot_general x1, matrix products, per_device(): lax.dot_general(whole_rows, lax.all_gather(encoder, 'prompt', axis=0, til...  7.26 us
  transfers between devices with their start and end apart: 2, of which 2 were waited for; matrix products, arithmetic and copies ran while one was open for 0% of the time, Pallas kernels for 0%

commit v1 on v0

--- a/solution.py
+++ b/solution.py
@@ -1,10 +1,19 @@
+import functools
+
 import jax
 import jax.numpy as jnp
 from jax import lax
+from jax.experimental import pallas as pl
+from jax.experimental.pallas import tpu as pltpu
 from jax.sharding import PartitionSpec as P
 
-
-def per_device(decoder, encoder, row_ids, counts, activity):
+MESH = pl.DeviceIdType.MESH
+LANES = 128
+COLUMNS = 2
+CORES = 2
+
+
+def gathered_encoder(decoder, encoder, row_ids, counts, activity):
     slot_count = row_ids.shape[1]
     owner_index = lax.axis_index("feat")
     picked_rows = jnp.take(decoder, row_ids[0], axis=0)
@@ -23,7 +32,225 @@
     return edges[None]
 
 
+X, Y, UP, DOWN, SIB = range(5)
+
+
+def kernel(
+    layers, ids_ref, counts_ref, act_ref, dec_hbm, enc_hbm, out_ref,
+    buf, dec, enc, act_other, part, local_sem, pair_send, pair_recv, send_sem, recv_sem,
+):
+    own, width = buf.shape[2], buf.shape[3]
+    targets = enc.shape[0]
+    slots = buf.shape[1] * own
+    half_width = width // LANES // 2 * LANES
+    spans = (pl.ds(0, half_width), pl.ds(half_width, width - half_width))
+
+    p = lax.axis_index("prompt")
+    f = lax.axis_index("feat")
+    core = f % CORES
+    y = (f // CORES) % COLUMNS
+    z = f // (CORES * COLUMNS)
+    q, yo = 1 - p, 1 - y
+
+    def owner(layer, column, which=None):
+        return (layer * COLUMNS + column) * CORES + (core if which is None else which)
+
+    places = {
+        X: (q, f),
+        Y: (p, owner(z, yo)),
+        UP: (p, owner(z + 1, y)),
+        DOWN: (p, owner(z - 1, y)),
+        SIB: (p, owner(z, y, 1 - core)),
+    }
+    inside = {UP: z < layers - 1, DOWN: z > 0}
+
+    load_dec = pltpu.make_async_copy(dec_hbm, dec, local_sem.at[0])
+    load_enc = pltpu.make_async_copy(enc_hbm, enc, local_sem.at[1])
+    load_dec.start()
+
+    barrier = pltpu.get_barrier_semaphore()
+    for way in (X, Y, SIB):
+        pl.semaphore_signal(barrier, inc=1, device_id=places[way], device_id_type=MESH)
+    for way in (UP, DOWN):
+        @pl.when(inside[way])
+        def _():
+            pl.semaphore_signal(barrier, inc=1, device_id=places[way], device_id_type=MESH)
+
+    row_count = dec.shape[0]
+    lane = lax.broadcasted_iota(jnp.int32, (own, row_count), 1)
+    slot = lax.broadcasted_iota(jnp.int32, (own, row_count), 0)
+    live = counts_ref[0, f]
+    wanted = jnp.full((own, row_count), -1, jnp.int32)
+    for k in range(own):
+        wanted = jnp.where(slot == k, jnp.where(k < live, ids_ref[0, k], -1), wanted)
+    one_hot = jnp.where(lane == wanted, 1.0, 0.0).astype(jnp.bfloat16)
+    load_dec.wait()
+    load_enc.start()
+    for span in spans:
+        picked = jnp.dot(one_hot, dec[:, span], preferred_element_type=jnp.float32)
+        buf[p, f, :, span] = picked.astype(buf.dtype)
+
+    peers = 3 + (z + layers - 1) // layers + (layers - 1 - z + layers - 1) // layers
+    pl.semaphore_wait(barrier, peers)
+
+    started = []
+
+    def piece(half, prompt, unit, way):
+        ref = buf.at[prompt, unit, :, spans[half]]
+        return pltpu.make_async_remote_copy(
+            src_ref=ref, dst_ref=ref,
+            send_sem=send_sem.at[way, half, prompt, unit],
+            recv_sem=recv_sem.at[half, prompt, unit],
+            device_id=places[way], device_id_type=MESH,
+        )
+
+    def send(half, prompt, unit, way, guard=None):
+        copy = piece(half, prompt, unit, way)
+        started.append((guard, copy))
+        if guard is None:
+            copy.start()
+        else:
+            pl.when(guard)(copy.start)
+
+    def arrived(half, prompt, unit):
+        piece(half, prompt, unit, SIB).wait_recv()
+
+    def both(a, b):
+        return jnp.logical_and(a, b)
+
+    act_copy = pltpu.make_async_remote_copy(
+        src_ref=act_ref, dst_ref=act_other, send_sem=pair_send.at[0], recv_sem=pair_recv.at[0],
+        device_id=places[X], device_id_type=MESH,
+    )
+    act_copy.start()
+
+    last = (X, Y)
+    send(0, p, f, Y)
+    send(1, p, f, X)
+    for way in (UP, DOWN):
+        for half in (0, 1):
+            send(half, p, f, way, inside[way])
+    send(0, p, f, X)
+    send(1, p, f, Y)
+    for half in (0, 1):
+        send(half, p, f, SIB)
+
+    for half, prompt, unit in ((0, p, owner(z, yo)), (1, q, f)):
+        arrived(half, prompt, unit)
+        for way in (UP, DOWN):
+            send(half, prompt, unit, way, inside[way])
+        send(half, prompt, unit, last[half])
+        send(half, prompt, unit, SIB)
+
+    def settle(layer, guard):
+        def run():
+            for half, prompt, column in ((0, q, y), (1, p, yo), (0, q, yo), (1, q, yo)):
+                arrived(half, prompt, owner(layer, column))
+                piece(half, prompt, owner(layer, column), SIB).start()
+        for half, prompt, column in ((0, q, y), (1, p, yo), (0, q, yo), (1, q, yo)):
+            started.append((guard, piece(half, prompt, owner(layer, column), SIB)))
+        if guard is None:
+            run()
+        else:
+            pl.when(guard)(run)
+
+    def sources(step):
+        return ((z - step, z - step >= 0, UP), (z + step, z + step < layers, DOWN))
+
+    for step in range(1, layers):
+        for half, prompt, column in ((0, p, y), (1, p, y), (0, p, yo), (1, q, y)):
+            for layer, present, way in sources(step):
+                unit = owner(layer, column)
+                pl.when(present)(functools.partial(arrived, half, prompt, unit))
+                send(half, prompt, unit, way, both(present, inside[way]))
+                send(half, prompt, unit, last[half], present)
+                send(half, prompt, unit, SIB, present)
+        if step == 1:
+            settle(z, None)
+        else:
+            for layer, present, _ in sources(step - 1):
+                settle(layer, present)
+    if layers == 1:
+        settle(z, None)
+    else:
+        for layer, present, _ in sources(layers - 1):
+            settle(layer, present)
+
+    def scale(weights):
+        return jnp.transpose(jnp.broadcast_to(weights[...], (LANES, slots)))[:, :1]
+
+    def product(prompt, weights):
+        rows = buf[prompt].reshape(slots, width)
+        sums = lax.dot_general(
+            rows, enc[...], (((1,), (1,)), ((), ())), preferred_element_type=jnp.float32
+        )
+        return (scale(weights) * sums).astype(out_ref.dtype)
+
+    def from_sibling(prompt):
+        for layer in range(layers):
+            for column in range(COLUMNS):
+                for half in (0, 1):
+                    arrived(half, prompt, owner(layer, column, 1 - core))
+
+    load_enc.wait()
+    act_copy.wait()
+    from_sibling(q)
+    part[...] = product(q, act_other)
+    mine = pl.ds(pl.multiple_of(p * targets, LANES), targets)
+    back = pltpu.make_async_remote_copy(
+        src_ref=part, dst_ref=out_ref.at[:, mine], send_sem=pair_send.at[1], recv_sem=pair_recv.at[1],
+        device_id=places[X], device_id_type=MESH,
+    )
+    back.start()
+    from_sibling(p)
+    out_ref[:, mine] = product(p, act_ref)
+    for guard, copy in started:
+        if guard is None:
+            copy.wait_send()
+        else:
+            pl.when(guard)(copy.wait_send)
+    back.wait()
+
+
+def moved_rows(prompts, owners, decoder, encoder, row_ids, counts, activity):
+    own, width, targets = row_ids.shape[1], decoder.shape[1], encoder.shape[0]
+    slots = owners * own
+    edges = pl.pallas_call(
+        functools.partial(kernel, owners // (COLUMNS * CORES)),
+        out_shape=jax.ShapeDtypeStruct((slots, prompts * targets), jnp.bfloat16),
+        in_specs=[
+            pl.BlockSpec(memory_space=pltpu.SMEM),
+            pl.BlockSpec(memory_space=pltpu.SMEM),
+            pl.BlockSpec(memory_space=pltpu.VMEM),
+            pl.BlockSpec(memory_space=pl.ANY),
+            pl.BlockSpec(memory_space=pl.ANY),
+        ],
+        out_specs=pl.BlockSpec(memory_space=pltpu.VMEM),
+        scratch_shapes=[
+            pltpu.VMEM((prompts, owners, own, width), decoder.dtype),
+            pltpu.VMEM(decoder.shape, decoder.dtype),
+            pltpu.VMEM(encoder.shape, encoder.dtype),
+            pltpu.VMEM(activity.shape, activity.dtype),
+            pltpu.VMEM((slots, targets), jnp.bfloat16),
+            pltpu.SemaphoreType.DMA((2,)),
+            pltpu.SemaphoreType.DMA((2,)),
+            pltpu.SemaphoreType.DMA((2,)),
+            pltpu.SemaphoreType.DMA((5, 2, prompts, owners)),
+            pltpu.SemaphoreType.DMA((2, prompts, owners)),
+        ],
+        compiler_params=pltpu.CompilerParams(
+            collective_id=0, has_side_effects=True, vmem_limit_bytes=48 * 1024 * 1024
+        ),
+    )(row_ids, counts, activity, decoder, encoder)
+    return edges[None]
+
+
 def solution(mesh):
+    prompts, owners = mesh.shape["prompt"], mesh.shape["feat"]
+    if prompts == 2 and owners % (COLUMNS * CORES) == 0:
+        per_device = functools.partial(moved_rows, prompts, owners)
+    else:
+        per_device = gathered_encoder
     in_specs = (
         P("feat", None),
         P(("feat", "prompt"), None),

time: 175 us -> 48.6 us (0.28)
  waiting for transfers between devices: 149 us -> 0 us
  Pallas kernels: 0 us -> 43.9 us
  between operations: 13.4 us -> 0.01 us
  matrix products: 7.26 us -> 0 us
  other arithmetic: 2.88 us -> 0 us
  local copies, waits for them, and re-layouts: 1.93 us -> 4.51 us
    all_gather x2 -> x0, waiting for transfers between devices: 148 us -> none  [the longest x1 103 us: per_device(): lax.all_gather(encoder, 'prompt', axis=0, tiled=True)]
    pallas_call x0 -> x1, Pallas kernels: none -> 43.9 us  [moved_rows(): pl.pallas_call(functools.partial(kernel, owners // (COLUMNS * CORES)), ou...]
    dot_general x1 -> x0, matrix products: 7.26 us -> none  [per_device(): lax.dot_general(whole_rows, lax.all_gather(encoder, 'prompt', axis=0, til...]
    unnamed x4 -> x9, local copies, waits for them, and re-layouts: 0.01 us -> 4.51 us
  transfers between devices with their start and end apart: 2 -> 0, of which waited for: 2 -> 0; matrix products, arithmetic and copies ran while one was open for 0% -> 0% of each run, Pallas kernels for 0% -> 0%
where the time goes in v1:
time: 48.6 us; the launch traced here: 48.4 us
  Pallas kernels  43.9 us (90%)
  local copies, waits for them, and re-layouts  4.51 us (9%)
    pallas_call x1, Pallas kernels, moved_rows(): pl.pallas_call(functools.partial(kernel, owners // (COLUMNS * CORES)), ou...  43.9 us
    unnamed x9, local copies, waits for them, and re-layouts  4.51 us

profile of v1, /device:TPU:0, one launch (start us, length us, event | category | flops | bytes accessed | tf_op | source)
XLA Modules:
  0.0 48.4 jit_solution(11543900442220349796)
XLA Ops:
  0.0 0.0 copy-start
  0.0 1.8 %copy-done = bf16[256,5376]{1,0:T(8,128)(2,1)S(1)} copy-done((bf16[256,5376]{1,0:T(8,128)(2,1)S(1)}, bf16[256,5376]{1,0:T(8,128)(2,1)}, u32[]{:S(2)}) %copy-start) | copy-done | bytes 2752536
  1.8 0.0 copy-start.1
  1.8 0.7 %copy-done.1 = f32[1,256]{1,0:T(1,128)S(1)} copy-done((f32[1,256]{1,0:T(1,128)S(1)}, f32[1,256]{1,0:T(1,128)}, u32[]{:S(2)}) %copy-start.1) | copy-done | bytes 1048
  2.5 0.0 copy-start.2
  2.5 0.7 %copy-done.2 = s32[1,16]{1,0:T(1,128)S(1)} copy-done((s32[1,16]{1,0:T(1,128)S(1)}, s32[1,16]{1,0:T(1,128)}, u32[]{:S(2)}) %copy-start.2) | copy-done | bytes 88
  3.1 0.0 copy-start.3
  3.1 0.7 %copy-done.3 = s32[1,16]{1,0:T(1,128)S(1)} copy-done((s32[1,16]{1,0:T(1,128)S(1)}, s32[1,16]{1,0:T(1,128)}, u32[]{:S(2)}) %copy-start.3) | copy-done | bytes 88
  3.8 43.9 %shard_map.55 = bf16[256,768]{1,0:T(8,128)(2,1)S(1)} custom-call(s32[1,16]{1,0:T(1,128)S(1)} %copy-done.2, s32[1,16]{1,0:T(1,128)S(1)} %copy-done.3, f32[1,256]{1,0:T(1,128)S(1)} %copy-done.1, bf16[256,5376]{1,0:T(8,128)(2,1)S(1)} %copy-done, bf16[384,5376]{1,0:T(8,128)(2,1)} %enc_hbm.1), custom_call_target="tpu_custom_call" | custom-call | tf_op jit(solution)/shard_map/pallas_call | solution.py:218
  47.7 0.7 %copy.7 = bf16[1,256,768]{2,1,0:T(8,128)(2,1)} copy(bf16[1,256,768]{2,1,0:T(8,128)(2,1)S(1)} %bitcast.1) | data formatting | bytes 786432
Async XLA Ops:
  0.0 1.8 %copy-start = (bf16[256,5376]{1,0:T(8,128)(2,1)S(1)}, bf16[256,5376]{1,0:T(8,128)(2,1)}, u32[]{:S(2)}) copy-start(bf16[256,5376]{1,0:T(8,128)(2,1)} %dec_hbm.1) | copy-start | bytes 8257540
  1.8 0.7 %copy-start.1 = (f32[1,256]{1,0:T(1,128)S(1)}, f32[1,256]{1,0:T(1,128)}, u32[]{:S(2)}) copy-start(f32[1,256]{1,0:T(1,128)} %act_ref.1) | copy-start | bytes 3076
  2.5 0.7 %copy-start.2 = (s32[1,16]{1,0:T(1,128)S(1)}, s32[1,16]{1,0:T(1,128)}, u32[]{:S(2)}) copy-start(s32[1,16]{1,0:T(1,128)} %ids_ref.1) | copy-start | bytes 196
  3.1 0.7 %copy-start.3 = (s32[1,16]{1,0:T(1,128)S(1)}, s32[1,16]{1,0:T(1,128)}, u32[]{:S(2)}) copy-start(s32[1,16]{1,0:T(1,128)} %counts_ref.1) | copy-start | bytes 196

commit v2 on v0

--- a/solution.py
+++ b/solution.py
@@ -1,10 +1,19 @@
+import functools
+
 import jax
 import jax.numpy as jnp
 from jax import lax
+from jax.experimental import pallas as pl
+from jax.experimental.pallas import tpu as pltpu
 from jax.sharding import PartitionSpec as P
 
-
-def per_device(decoder, encoder, row_ids, counts, activity):
+MESH = pl.DeviceIdType.MESH
+LANES = 128
+COLUMNS = 2
+CORES = 2
+
+
+def gathered_encoder(decoder, encoder, row_ids, counts, activity):
     slot_count = row_ids.shape[1]
     owner_index = lax.axis_index("feat")
     picked_rows = jnp.take(decoder, row_ids[0], axis=0)
@@ -23,7 +32,245 @@
     return edges[None]
 
 
+X, Y, UP, DOWN, SIB = range(5)
+
+
+def kernel(
+    layers, ids_hbm, counts_hbm, act_hbm, dec_hbm, enc_hbm, out_ref,
+    buf, dec, enc, ids, counts, act, scale, part,
+    small_sem, load_sem, act_send, act_recv, back_send, back_recv, send_sem, recv_sem,
+):
+    prompts, members, own, width = buf.shape[1:]
+    targets = enc.shape[0]
+    layer_slots = members * own
+    half_width = width // LANES // 2 * LANES
+    spans = (pl.ds(0, half_width), pl.ds(half_width, width - half_width))
+
+    p = lax.axis_index("prompt")
+    f = lax.axis_index("feat")
+    core = f % CORES
+    y = (f // CORES) % COLUMNS
+    z = f // (CORES * COLUMNS)
+    q, yo = 1 - p, 1 - y
+
+    def owner(layer, column, which):
+        return (layer * COLUMNS + column) * CORES + which
+
+    places = {
+        X: (q, f),
+        Y: (p, owner(z, yo, core)),
+        UP: (p, owner(z + 1, y, core)),
+        DOWN: (p, owner(z - 1, y, core)),
+        SIB: (p, owner(z, y, 1 - core)),
+    }
+    inside = {UP: z < layers - 1, DOWN: z > 0}
+
+    load_small = [
+        pltpu.make_async_copy(src, dst, small_sem.at[i])
+        for i, (src, dst) in enumerate(((ids_hbm, ids), (counts_hbm, counts), (act_hbm, act.at[0])))
+    ]
+    load_dec = [
+        pltpu.make_async_copy(dec_hbm.at[:, span], dec.at[:, span], load_sem.at[i])
+        for i, span in enumerate(spans)
+    ]
+    load_enc = pltpu.make_async_copy(enc_hbm, enc, load_sem.at[2])
+    for copy in load_small + load_dec:
+        copy.start()
+
+    barrier = pltpu.get_barrier_semaphore()
+    for way in (X, Y, SIB):
+        pl.semaphore_signal(barrier, inc=1, device_id=places[way], device_id_type=MESH)
+    for way in (UP, DOWN):
+        @pl.when(inside[way])
+        def _():
+            pl.semaphore_signal(barrier, inc=1, device_id=places[way], device_id_type=MESH)
+
+    for copy in load_small:
+        copy.wait()
+    row_count = dec.shape[0]
+    lane = lax.broadcasted_iota(jnp.int32, (own, row_count), 1)
+    slot = lax.broadcasted_iota(jnp.int32, (own, row_count), 0)
+    live = counts[0, f]
+    wanted = jnp.full((own, row_count), -1, jnp.int32)
+    for k in range(own):
+        wanted = jnp.where(slot == k, jnp.where(k < live, ids[0, k], -1), wanted)
+    one_hot = jnp.where(lane == wanted, 1.0, 0.0).astype(jnp.bfloat16)
+
+    def pick(half):
+        load_dec[half].wait()
+        rows = jnp.dot(one_hot, dec[:, spans[half]], preferred_element_type=jnp.float32)
+        buf[z, p, y * CORES + core, :, spans[half]] = rows.astype(buf.dtype)
+
+    started = []
+
+    def piece(half, prompt, layer, column, way, which=None):
+        member = column * CORES + (core if which is None else which)
+        ref = buf.at[layer, prompt, member, :, spans[half]]
+        return pltpu.make_async_remote_copy(
+            src_ref=ref, dst_ref=ref,
+            send_sem=send_sem.at[way, half, layer, prompt, member],
+            recv_sem=recv_sem.at[half, layer, prompt, member],
+            device_id=places[way], device_id_type=MESH,
+        )
+
+    def send(half, prompt, layer, column, way, guard=None):
+        copy = piece(half, prompt, layer, column, way)
+        started.append((guard, copy))
+        if guard is None:
+            copy.start()
+        else:
+            pl.when(guard)(copy.start)
+
+    def arrived(half, prompt, layer, column, which=None):
+        piece(half, prompt, layer, column, SIB, which).wait_recv()
+
+    def both(a, b):
+        return jnp.logical_and(a, b)
+
+    first, last = (Y, X), (X, Y)
+
+    def launch(half):
+        for way in (UP, DOWN):
+            send(half, p, z, y, way, inside[way])
+        send(half, p, z, y, first[half])
+        send(half, p, z, y, last[half])
+        send(half, p, z, y, SIB)
+
+    pick(0)
+    load_enc.start()
+    peers = 3 + (z + layers - 1) // layers + (layers - 1 - z + layers - 1) // layers
+    pl.semaphore_wait(barrier, peers)
+    launch(0)
+    pick(1)
+    launch(1)
+    act_copy = pltpu.make_async_remote_copy(
+        src_ref=act.at[0], dst_ref=act.at[1], send_sem=act_send.at[0], recv_sem=act_recv.at[0],
+        device_id=places[X], device_id_type=MESH,
+    )
+    act_copy.start()
+
+    for half, prompt, column in ((0, p, yo), (1, q, y)):
+        arrived(half, prompt, z, column)
+        for way in (UP, DOWN):
+            send(half, prompt, z, column, way, inside[way])
+        send(half, prompt, z, column, last[half])
+        send(half, prompt, z, column, SIB)
+
+    for i in (0, 1):
+        if i == 1:
+            act_copy.wait()
+        row = jnp.broadcast_to(act[i], (LANES, act.shape[2]))
+        scale[i] = jnp.transpose(row)
+    load_enc.wait()
+
+    def sources(step):
+        if step == 0:
+            return ((z, None, None),)
+        return ((z - step, z - step >= 0, UP), (z + step, z + step < layers, DOWN))
+
+    def guarded(guard, run):
+        if guard is None:
+            run()
+        else:
+            pl.when(guard)(run)
+
+    def settle(step):
+        for layer, present, _ in sources(step):
+            for half, prompt, column in ((0, q, y), (1, p, yo), (0, q, yo), (1, q, yo)):
+                guarded(present, functools.partial(arrived, half, prompt, layer, column))
+                send(half, prompt, layer, column, SIB, present)
+
+    mine = pl.ds(pl.multiple_of(p * targets, LANES), targets)
+
+    def back(layer):
+        rows = pl.ds(pl.multiple_of(layer * layer_slots, layer_slots), layer_slots)
+        return pltpu.make_async_remote_copy(
+            src_ref=part.at[rows], dst_ref=out_ref.at[rows, mine],
+            send_sem=back_send.at[layer], recv_sem=back_recv.at[layer],
+            device_id=places[X], device_id_type=MESH,
+        )
+
+    def multiply(layer):
+        for prompt in (q, p):
+            for column in range(COLUMNS):
+                for half in (0, 1):
+                    arrived(half, prompt, layer, column, 1 - core)
+        rows = pl.ds(pl.multiple_of(layer * layer_slots, layer_slots), layer_slots)
+        sums = lax.dot_general(
+            buf[layer].reshape(prompts * layer_slots, width), enc[...],
+            (((1,), (1,)), ((), ())), preferred_element_type=jnp.float32,
+        )
+        lower, upper = sums[:layer_slots], sums[layer_slots:]
+        here = jnp.where(p == 0, lower, upper)
+        there = jnp.where(p == 0, upper, lower)
+        part[rows, :] = (scale[1, rows, :1] * there).astype(part.dtype)
+        back(layer).start()
+        out_ref[rows, mine] = (scale[0, rows, :1] * here).astype(out_ref.dtype)
+
+    def compute(step):
+        for layer, present, _ in sources(step):
+            guarded(present, functools.partial(multiply, layer))
+
+    for step in range(1, layers):
+        for n, (half, prompt, column) in enumerate(((0, p, y), (1, p, y), (0, p, yo), (1, q, y))):
+            for layer, present, way in sources(step):
+                pl.when(present)(functools.partial(arrived, half, prompt, layer, column))
+                send(half, prompt, layer, column, way, both(present, inside[way]))
+                send(half, prompt, layer, column, last[half], present)
+                send(half, prompt, layer, column, SIB, present)
+            if n == 1:
+                settle(step - 1)
+            if n == 2:
+                compute(step - 1)
+    settle(layers - 1)
+    compute(layers - 1)
+
+    for guard, copy in started:
+        guarded(guard, copy.wait_send)
+    for layer in range(layers):
+        back(layer).wait()
+
+
+def moved_rows(prompts, owners, decoder, encoder, row_ids, counts, activity):
+    own, width, targets = row_ids.shape[1], decoder.shape[1], encoder.shape[0]
+    members = COLUMNS * CORES
+    layers, slots = owners // members, owners * own
+    edges = pl.pallas_call(
+        functools.partial(kernel, layers),
+        out_shape=jax.ShapeDtypeStruct((slots, prompts * targets), jnp.bfloat16),
+        in_specs=[pl.BlockSpec(memory_space=pl.ANY)] * 5,
+        out_specs=pl.BlockSpec(memory_space=pltpu.VMEM),
+        scratch_shapes=[
+            pltpu.VMEM((layers, prompts, members, own, width), decoder.dtype),
+            pltpu.VMEM(decoder.shape, decoder.dtype),
+            pltpu.VMEM(encoder.shape, encoder.dtype),
+            pltpu.SMEM(row_ids.shape, row_ids.dtype),
+            pltpu.SMEM(counts.shape, counts.dtype),
+            pltpu.VMEM((prompts,) + activity.shape, activity.dtype),
+            pltpu.VMEM((prompts, slots, LANES), activity.dtype),
+            pltpu.VMEM((slots, targets), jnp.bfloat16),
+            pltpu.SemaphoreType.DMA((3,)),
+            pltpu.SemaphoreType.DMA((3,)),
+            pltpu.SemaphoreType.DMA((1,)),
+            pltpu.SemaphoreType.DMA((1,)),
+            pltpu.SemaphoreType.DMA((layers,)),
+            pltpu.SemaphoreType.DMA((layers,)),
+            pltpu.SemaphoreType.DMA((5, 2, layers, prompts, members)),
+            pltpu.SemaphoreType.DMA((2, layers, prompts, members)),
+        ],
+        compiler_params=pltpu.CompilerParams(
+            collective_id=0, has_side_effects=True, vmem_limit_bytes=58 * 1024 * 1024
+        ),
+    )(row_ids, counts, activity, decoder, encoder)
+    return edges[None]
+
+
 def solution(mesh):
+    prompts, owners = mesh.shape["prompt"], mesh.shape["feat"]
+    if prompts == 2 and owners % (COLUMNS * CORES) == 0:
+        per_device = functools.partial(moved_rows, prompts, owners)
+    else:
+        per_device = gathered_encoder
     in_specs = (
         P("feat", None),
         P(("feat", "prompt"), None),

time: 175 us -> 44.4 us (0.25)
  waiting for transfers between devices: 149 us -> 0 us
  Pallas kernels: 0 us -> 42.4 us
  between operations: 13.4 us -> 0.01 us
  matrix products: 7.26 us -> 0 us
  other arithmetic: 2.88 us -> 0 us
    all_gather x2 -> x0, waiting for transfers between devices: 148 us -> none  [the longest x1 103 us: per_device(): lax.all_gather(encoder, 'prompt', axis=0, tiled=True)]
    pallas_call x0 -> x1, Pallas kernels: none -> 42.4 us  [moved_rows(): pl.pallas_call(functools.partial(kernel, layers), out_shape=jax.ShapeDtyp...]
    dot_general x1 -> x0, matrix products: 7.26 us -> none  [per_device(): lax.dot_general(whole_rows, lax.all_gather(encoder, 'prompt', axis=0, til...]
    unnamed x4 -> x1, local copies, waits for them, and re-layouts: 0.01 us -> 1.77 us
  transfers between devices with their start and end apart: 2 -> 0, of which waited for: 2 -> 0; matrix products, arithmetic and copies ran while one was open for 0% -> 0% of each run, Pallas kernels for 0% -> 0%
where the time goes in v2:
time: 44.4 us; the launch traced here: 44.2 us
  Pallas kernels  42.4 us (95%)
  local copies, waits for them, and re-layouts  1.77 us (4%)
    pallas_call x1, Pallas kernels, moved_rows(): pl.pallas_call(functools.partial(kernel, layers), out_shape=jax.ShapeDtyp...  42.4 us
    unnamed x1, local copies, waits for them, and re-layouts  1.77 us

profile of v2, /device:TPU:0, one launch (start us, length us, event | category | flops | bytes accessed | tf_op | source)
XLA Modules:
  0.0 44.2 jit_solution(9479186022477405782)
XLA Ops:
  0.0 42.4 %shard_map.55 = bf16[256,768]{1,0:T(8,128)(2,1)} custom-call(s32[1,16]{1,0:T(1,128)} %ids_hbm.1, s32[1,16]{1,0:T(1,128)} %counts_hbm.1, f32[1,256]{1,0:T(1,128)} %act_hbm.1, bf16[256,5376]{1,0:T(8,128)(2,1)} %dec_hbm.1, bf16[384,5376]{1,0:T(8,128)(2,1)} %enc_hbm.1), custom_call_target="tpu_custom_call" | custom-call | tf_op jit(solution)/shard_map/pallas_call | solution.py:238
  42.4 1.8 %copy.7 = bf16[1,256,768]{2,1,0:T(8,128)(2,1)} copy(bf16[1,256,768]{2,1,0:T(8,128)(2,1)} %bitcast.1) | data formatting | bytes 786432

commit v3 on v2

--- a/solution.py
+++ b/solution.py
@@ -212,16 +212,14 @@
             guarded(present, functools.partial(multiply, layer))
 
     for step in range(1, layers):
-        for n, (half, prompt, column) in enumerate(((0, p, y), (1, p, y), (0, p, yo), (1, q, y))):
+        for half, prompt, column in ((0, p, y), (1, p, y), (0, p, yo), (1, q, y)):
             for layer, present, way in sources(step):
                 pl.when(present)(functools.partial(arrived, half, prompt, layer, column))
                 send(half, prompt, layer, column, way, both(present, inside[way]))
                 send(half, prompt, layer, column, last[half], present)
                 send(half, prompt, layer, column, SIB, present)
-            if n == 1:
-                settle(step - 1)
-            if n == 2:
-                compute(step - 1)
+        settle(step - 1)
+        compute(step - 1)
     settle(layers - 1)
     compute(layers - 1)
 

time: 44.4 us -> 42.6 us (0.959)
  Pallas kernels: 42.4 us -> 40.7 us
    pallas_call x1, Pallas kernels: 42.4 us -> 40.7 us  [moved_rows(): pl.pallas_call(functools.partial(kernel, layers), out_shape=jax.ShapeDtyp...]
where the time goes in v3:
time: 42.6 us; the launch traced here: 42.4 us
  Pallas kernels  40.7 us (96%)
  local copies, waits for them, and re-layouts  1.77 us (4%)
    pallas_call x1, Pallas kernels, moved_rows(): pl.pallas_call(functools.partial(kernel, layers), out_shape=jax.ShapeDtyp...  40.7 us
    unnamed x1, local copies, waits for them, and re-layouts  1.77 us

profile of v3, /device:TPU:0, one launch (start us, length us, event | category | flops | bytes accessed | tf_op | source)
XLA Modules:
  0.0 42.4 jit_solution(16976688301346877041)
XLA Ops:
  0.0 40.7 %shard_map.55 = bf16[256,768]{1,0:T(8,128)(2,1)} custom-call(s32[1,16]{1,0:T(1,128)} %ids_hbm.1, s32[1,16]{1,0:T(1,128)} %counts_hbm.1, f32[1,256]{1,0:T(1,128)} %act_hbm.1, bf16[256,5376]{1,0:T(8,128)(2,1)} %dec_hbm.1, bf16[384,5376]{1,0:T(8,128)(2,1)} %enc_hbm.1), custom_call_target="tpu_custom_call" | custom-call | tf_op jit(solution)/shard_map/pallas_call | solution.py:236
  40.7 1.8 %copy.7 = bf16[1,256,768]{2,1,0:T(8,128)(2,1)} copy(bf16[1,256,768]{2,1,0:T(8,128)(2,1)} %bitcast.1) | data formatting | bytes 786432

commit v4 on v3

--- a/solution.py
+++ b/solution.py
@@ -207,9 +207,26 @@
         back(layer).start()
         out_ref[rows, mine] = (scale[0, rows, :1] * here).astype(out_ref.dtype)
 
+    def multiply_apart(layer):
+        rows = pl.ds(pl.multiple_of(layer * layer_slots, layer_slots), layer_slots)
+        for prompt in (q, p):
+            for column in range(COLUMNS):
+                for half in (0, 1):
+                    arrived(half, prompt, layer, column, 1 - core)
+            sums = lax.dot_general(
+                buf[layer, prompt].reshape(layer_slots, width), enc[...],
+                (((1,), (1,)), ((), ())), preferred_element_type=jnp.float32,
+            )
+            if prompt is q:
+                part[rows, :] = (scale[1, rows, :1] * sums).astype(part.dtype)
+                back(layer).start()
+            else:
+                out_ref[rows, mine] = (scale[0, rows, :1] * sums).astype(out_ref.dtype)
+
     def compute(step):
+        run = multiply_apart if step == layers - 1 else multiply
         for layer, present, _ in sources(step):
-            guarded(present, functools.partial(multiply, layer))
+            guarded(present, functools.partial(run, layer))
 
     for step in range(1, layers):
         for half, prompt, column in ((0, p, y), (1, p, y), (0, p, yo), (1, q, y)):

time: 42.6 us -> 43 us (level)
  no operation moved by 1% of the time
where the time goes in v4:
time: 43 us; the launch traced here: 42.8 us
  Pallas kernels  41 us (95%)
  local copies, waits for them, and re-layouts  1.77 us (4%)
    pallas_call x1, Pallas kernels, moved_rows(): pl.pallas_call(functools.partial(kernel, layers), out_shape=jax.ShapeDtyp...  41 us
    unnamed x1, local copies, waits for them, and re-layouts  1.77 us

profile of v4, /device:TPU:0, one launch (start us, length us, event | category | flops | bytes accessed | tf_op | source)
XLA Modules:
  0.0 42.8 jit_solution(18408252259094097815)
XLA Ops:
  0.0 41.0 %shard_map.55 = bf16[256,768]{1,0:T(8,128)(2,1)} custom-call(s32[1,16]{1,0:T(1,128)} %ids_hbm.1, s32[1,16]{1,0:T(1,128)} %counts_hbm.1, f32[1,256]{1,0:T(1,128)} %act_hbm.1, bf16[256,5376]{1,0:T(8,128)(2,1)} %dec_hbm.1, bf16[384,5376]{1,0:T(8,128)(2,1)} %enc_hbm.1), custom_call_target="tpu_custom_call" | custom-call | tf_op jit(solution)/shard_map/pallas_call | solution.py:253
  41.0 1.8 %copy.7 = bf16[1,256,768]{2,1,0:T(8,128)(2,1)} copy(bf16[1,256,768]{2,1,0:T(8,128)(2,1)} %bitcast.1) | data formatting | bytes 786432
